TPU v7x, 32 devices: a whole 2x2x4 slice. The times are simulated.
32 devices in a mesh: chan: 8 (over z, y), ctx: 4 (over x, core).
Axes of the slice: x: 2, y: 2, z: 4, core: 2. Of those that a mesh axis runs over, the one named last changes fastest.
Arguments:
- query_in: bfloat16 [6144, 8192], P('ctx', 'chan'), may hold values from -6 to 6
- key_in: bfloat16 [6144, 8192], P('ctx', 'chan'), may hold values from -6 to 6
- value_in: bfloat16 [6144, 8192], P('ctx', 'chan'), may hold values from -6 to 6
- short_filter: float32 [3, 3, 8192], P(None, None, 'chan'), may hold values from -3.5 to 3.5
- residue: float32 [8192, 16], P('chan'), may hold values from -1.5 to 1.5
- decay_rate: float32 [8192, 16], P('chan'), may hold values from 3.25520833e-05 to 0.0333333333, as said below
- skip_gain: float32 [8192], P('chan'), may hold values from -4 to 4
- out_weight: bfloat16 [8192, 8192], P('ctx', 'chan'), may hold values from -0.0625 to 0.0625
Outputs:
- mixed_out: bfloat16 [6144, 8192], P('ctx', 'chan')
Inputs may be any that keep to these rules, and one draw needn't show every extreme that they name: `decay_rate`: rates of the filter's modes.
All inputs are finite; a program needn't handle non-finite values.
Results may differ from a plain program's by a relative error of at most 0.0051.
Values may be sent and summed in bfloat16 or wider, within the bound.
A program may use at most 256 MiB of HBM per device.

v0:
```python
import jax
import jax.numpy as jnp
from jax import lax
from jax.sharding import PartitionSpec as P

HIGHEST = lax.Precision.HIGHEST


def from_behind(value, axis, by):
    devices = lax.axis_size(axis)
    pairs = [(i, i + by) for i in range(devices) if 0 <= i + by < devices]
    return lax.ppermute(value, axis, pairs)


def short_pass(padded, short_filter, length_all):
    tap_count = short_filter.shape[1]
    result = jnp.zeros((padded.shape[0], length_all, padded.shape[2]), jnp.float32)
    for tap_index in range(tap_count):
        begin = tap_count - 1 - tap_index
        result = (
            result + short_filter[:, tap_index, None, :] * padded[:, begin : begin + length_all, :]
        )
    return result


def on_device(query_in, key_in, value_in, short_filter, residue, decay_rate, skip_gain, out_weight):
    tokens = query_in.shape[0]
    channels = query_in.shape[1]
    tap_count = short_filter.shape[1]
    stacked = jnp.stack([query_in, key_in, value_in])
    boundary = from_behind(stacked[:, tokens - (tap_count - 1) :, :], "ctx", 1)
    padded = jnp.concatenate([boundary, stacked], axis=1).astype(jnp.float32)
    shorted = short_pass(padded, short_filter, tokens)
    drive_in = shorted[1] * shorted[2]
    block_len = min(64, tokens)
    block_count = tokens // block_len
    mode_gain = residue * jnp.sqrt(decay_rate)
    offsets = jnp.arange(block_len, dtype=jnp.float32)
    powers = jnp.exp(-decay_rate[None] * offsets[:, None, None])
    kernel = jnp.sum(powers * mode_gain[None], axis=2)
    positions = jnp.arange(block_len)
    lag_matrix = positions[:, None] - positions[None, :]
    toeplitz = jnp.where(
        (lag_matrix >= 0)[:, :, None], jnp.take(kernel, jnp.maximum(lag_matrix, 0), axis=0), 0.0
    )
    blocks = drive_in.reshape(block_count, block_len, channels)
    within = jnp.einsum("tsc,bsc->btc", toeplitz, blocks, precision=HIGHEST)
    tail_decay = jnp.exp(-decay_rate[None] * (block_len - 1.0 - offsets)[:, None, None])
    block_ends = jnp.einsum("bsc,scn->bcn", blocks, tail_decay, precision=HIGHEST)
    block_index = jnp.arange(block_count)
    distance = block_index[:, None] - 1 - block_index[None, :]
    steps_back = (block_len * jnp.maximum(distance, 0)).astype(jnp.float32)
    carry_weight = jnp.where(
        (distance >= 0)[:, :, None, None],
        jnp.exp(-decay_rate[None, None] * steps_back[:, :, None, None]),
        0.0,
    )
    prefix = jnp.einsum("abcn,bcn->acn", carry_weight, block_ends, precision=HIGHEST)
    local_end = jnp.exp(-decay_rate * block_len) * prefix[-1] + block_ends[-1]
    end_states = lax.all_gather(local_end[None], "ctx", axis=0, tiled=True)
    ctx_count = lax.axis_size("ctx")
    position = lax.axis_index("ctx")
    sources = jnp.arange(ctx_count)
    hops = position - 1 - sources
    hop_span = (tokens * jnp.maximum(hops, 0)).astype(jnp.float32)
    source_weight = jnp.where(
        (hops >= 0)[:, None, None], jnp.exp(-decay_rate[None] * hop_span[:, None, None]), 0.0
    )
    carry_in = jnp.sum(source_weight * end_states, axis=0)
    entry_decay = jnp.exp(
        -decay_rate[None] * (block_len * block_index).astype(jnp.float32)[:, None, None]
    )
    state_in = prefix + entry_decay * carry_in[None]
    lead_decay = jnp.exp(-decay_rate[None] * (offsets + 1.0)[:, None, None]) * mode_gain[None]
    across = jnp.einsum("tcn,bcn->btc", lead_decay, state_in, precision=HIGHEST)
    mode_conv = (within + across).reshape(tokens, channels)
    gated_out = (shorted[0] * (mode_conv + skip_gain[None, :] * drive_in)).astype(jnp.bfloat16)
    weight_cols = lax.all_gather(out_weight, "ctx", axis=0, tiled=True)
    mixed_out = jnp.dot(
        lax.all_gather(gated_out, "chan", axis=1, tiled=True),
        weight_cols,
        preferred_element_type=jnp.float32,
    )
    return mixed_out.astype(jnp.bfloat16)


def solution(mesh):
    in_specs = (
        P("ctx", "chan"),
        P("ctx", "chan"),
        P("ctx", "chan"),
        P(None, None, "chan"),
        P("chan", None),
        P("chan", None),
        P("chan"),
        P("ctx", "chan"),
    )
    out_specs = P("ctx", "chan")
    return jax.shard_map(
        on_device, mesh=mesh, in_specs=in_specs, out_specs=out_specs, check_vma=False
    )
```

profile of v0, /device:TPU:0, one launch (start us, length us, event | category | flops | bytes accessed | tf_op | source)
XLA Modules:
  0.0 816.3 jit_solution(11897876534222370192)
XLA Ops:
  6.5 0.7 all-gather.6.cloned.1.call-update
  7.3 0.8 pad_maximum_fusion
  8.1 2.4 collective-permute-start
  10.6 0.1 fusion.29
  10.9 0.2 copy.35
  11.1 0.2 collective-permute-done
  11.3 6.4 maximum_convert_fusion
  17.7 11.7 %fusion.3 = f32[3,1536,1024]{2,1,0:T(8,128)} fusion(f32[3,1538,1024]{2,1,0:T(8,128)S(1)} %maximum_convert_fusion, f32[3,1024]{1,0:T(4,128)S(1)} %get-tuple-element.10, f32[3,1024]{1,0:T(4,128)S(1)} %get-tuple-element.11, f32[3,1024]{1,0:T(4,128)S(1)} %bitcast.65), kind=kLoop, calls=%fused_computation.6 | loop fusion | flops 23592960 | bytes 75534336 | tf_op jit(solution)/shard_map/add | solution.py:21
  29.4 9.8 %slice_multiply_fusion.3 = f32[1,1536,1024]{2,1,0:T(8,128)} fusion(f32[3,1536,1024]{2,1,0:T(8,128)} %fusion.3), kind=kLoop, calls=%fused_computation.24 | loop fusion | flops 1572864 | bytes 18874368 | tf_op jit(solution)/shard_map/mul | solution.py:34
  39.1 9.7 %copy.39 = f32[24,64,1024]{1,0,2:T(8,128)} copy(f32[24,64,1024]{2,1,0:T(8,128)} %bitcast.57) | data formatting | bytes 12582912 | tf_op jit(solution)/shard_map/mul | solution.py:34
  48.9 24.5 %fusion.13 = f32[1024,16,24]{2,1,0:T(8,128)} fusion(f32[24,64,1024]{1,0,2:T(8,128)} %copy.39, f32[64]{0:T(128)S(1)} %iota_subtract_fusion.3, f32[1024,16]{1,0:T(8,128)S(1)} %copy.35), kind=kOutput, calls=%fused_computation.20 | convolution fusion | flops 303038464 | bytes 7930112 | tf_op jit(solution)/shard_map/bsc,scn->bcn/dot_general | solution.py:49
  73.4 6.0 copy.54
  79.4 9.0 %slice.57 = f32[1,1024,16]{0,2,1:T(8,128)} slice(f32[24,1024,16]{0,2,1:T(8,128)} %bitcast.55), slice={[23:24], [0:1024], [0:16]} | slice | bytes 131072 | tf_op jit(solution)/shard_map/slice | solution.py:59
  88.4 5.2 copy.41
  93.7 11.6 %multiply_reduce_fusion = f32[1024,16,24]{0,1,2:T(8,128)S(1)} fusion(f32[1024,16,24]{0,1,2:T(8,128)S(1)} %copy.54, f32[24,24]{1,0:T(8,128)S(1)} %multiply_convert_fusion, f32[1024,16]{0,1:T(8,128)S(1)} %neg.4, pred[24,24]{1,0:T(8,128)(4,1)S(1)} %fusion.29), kind=kLoop, calls=%fused_computation.1 | loop fusion | flops 37355520 | bytes 3214144 | tf_op jit(solution)/shard_map/abcn,bcn->acn/dot_general | solution.py:58
  105.3 1.1 copy-done.1
  106.4 0.2 copy.36
  106.6 11.7 %multiply_reduce_fusion.1 = f32[64,1024]{0,1:T(8,128)S(1)} fusion(f32[1024,16]{1,0:T(8,128)S(1)} %copy.36, f32[1024,16]{1,0:T(8,128)S(1)} %copy.35), kind=kLoop, calls=%fused_computation.23 | loop fusion | flops 3080192 | bytes 393216 | tf_op jit(solution)/shard_map/reduce_sum | solution.py:40
  118.3 0.2 copy.37
  118.5 18.5 %gather_fusion = f32[4096,1024]{1,0:T(8,128)} fusion(f32[64,1024]{1,0:T(8,128)S(1)} %copy.37, s32[4096]{0:T(1024)S(1)} %broadcast_clamp_fusion), kind=kCustom, calls=%fused_computation | custom fusion | bytes 33570816 | tf_op jit(solution)/shard_map/jit(_take)/gather | solution.py:44
  137.1 30.5 %copy.38 = f32[64,64,1024]{1,0,2:T(8,128)} copy(f32[64,64,1024]{2,1,0:T(8,128)} %bitcast.56) | data formatting | bytes 33554432 | tf_op jit(solution)/shard_map/jit(_take)/gather | solution.py:44
  167.5 8.3 %all-gather = f32[4096,16]{0,1:T(8,128)S(1)} all-gather(f32[1024,16]{0,1:T(8,128)S(1)} %get-tuple-element.5), channel_id=2, replica_groups=mesh['chan'=8,'ctx'=4] {'ctx'}, dimensions={0}, use_global_device_ids=true | all-gather | bytes 327680 | tf_op jit(solution)/shard_map/all_gather | solution.py:60
  175.8 0.2 reshape.137
  176.0 0.3 multiply_reduce_fusion.2
  176.3 1.7 multiply_add_fusion
  178.0 6.6 copy.42
  184.6 58.4 %fusion = f32[1024,24,64]{2,1,0:T(8,128)S(1)} fusion(f32[24,64,1024]{1,0,2:T(8,128)} %copy.39, f32[64,64,1024]{1,0,2:T(8,128)} %copy.38, pred[64,64]{1,0:T(8,128)(4,1)S(1)} %get-tuple-element.12, pred[64,64]{1,0:T(8,128)(4,1)S(1)} %get-tuple-element.13), kind=kOutput, calls=%fused_computation.2 | convolution fusion | flops 1216348160 | bytes 29368320 | tf_op jit(solution)/shard_map/tsc,bsc->btc/dot_general | solution.py:47
  243.0 29.6 %add_bitcast_fusion = f32[24,64,1024]{1,0,2:T(8,128)} fusion(f32[1024,24,64]{2,1,0:T(8,128)S(1)} %fusion, f32[24,1024,16]{0,2,1:T(8,128)S(1)} %copy-done, f32[64]{0:T(128)S(1)} %iota_add_fusion, f32[1024,16]{1,0:T(8,128)S(1)} %copy.36, f32[1024,16]{1,0:T(8,128)S(1)} %copy.35), kind=kOutput, calls=%fused_computation.14 | convolution fusion | flops 305659904 | bytes 14287104 | tf_op jit(solution)/shard_map/tcn,bcn->btc/dot_general | solution.py:75
  272.7 9.8 %copy.43 = f32[24,64,1024]{2,1,0:T(8,128)} copy(f32[24,64,1024]{1,0,2:T(8,128)} %add_bitcast_fusion) | data formatting | bytes 12582912 | tf_op jit(solution)/shard_map/add | solution.py:76
  282.5 11.5 %fusion.17 = bf16[1536,1024]{1,0:T(8,128)(2,1)} fusion(f32[3,1536,1024]{2,1,0:T(8,128)} %fusion.3, f32[24,64,1024]{2,1,0:T(8,128)} %copy.43, f32[1024]{0:T(1024)S(1)} %copy-done.5), kind=kLoop, calls=%fused_computation.27 | loop fusion | flops 7864320 | bytes 28315648 | tf_op jit(solution)/shard_map/convert_element_type | solution.py:77
  294.0 482.0 %all-gather.4.cloned.1.call-done = bf16[1536,8192]{1,0:T(8,128)(2,1)} async-done(((bf16[1536,1024]{1,0:T(8,128)(2,1)}), bf16[1536,8192]{1,0:T(8,128)(2,1)}) %all-gather.4.cloned.1.call-update) | async-done | bytes 25165840 | tf_op jit(solution)/shard_map/all_gather | solution.py:80
  776.0 33.0 %convolution_convert_fusion = bf16[1536,1024]{1,0:T(8,128)(2,1)} fusion(bf16[1536,8192]{1,0:T(8,128)(2,1)} %all-gather.4.cloned.1.call-done, bf16[8192,1024]{1,0:T(8,128)(2,1)} %all-gather.6.cloned.1.call-done), kind=kOutput, calls=%fused_computation.35 | convolution fusion | flops 25771376640 | bytes 45088768 | tf_op jit(solution)/shard_map/dot_general | solution.py:79
  (31 shorter events, 0.4 us)
Async XLA Ops:
  6.5 4.2 copy-start.4
  6.5 4.3 copy-start.2
  6.5 287.5 %all-gather.6.cloned.1.call-start = ((), (), s32[]{:S(2)}) async-start(), calls=%async_computation.1 | async-start | bytes 20971520 | tf_op jit(solution)/shard_map/all_gather | solution.py:78
  7.3 768.7 %all-gather.4.cloned.1.call-start = ((), (), s32[]{:S(2)}) async-start(), calls=%async_computation | async-start | bytes 28311552 | tf_op jit(solution)/shard_map/all_gather | solution.py:80
  8.1 3.2 collective-permute-start
  93.7 11.6 %copy-start.3 = (f32[1024,16]{0,1:T(8,128)S(1)}, f32[1024,16]{0,1:T(8,128)}, u32[]{:S(2)}) copy-start(f32[1024,16]{0,1:T(8,128)} %param.12) | copy-start | bytes 196612
  105.2 1.1 copy-start.1
  184.6 58.4 %copy-start = (f32[24,1024,16]{0,2,1:T(8,128)S(1)}, f32[24,1024,16]{0,2,1:T(8,128)}, u32[]{:S(2)}) copy-start(f32[24,1024,16]{0,2,1:T(8,128)} %copy.42) | copy-start | bytes 4718596
  272.7 9.8 %copy-start.5 = (f32[1024]{0:T(1024)S(1)}, f32[1024]{0:T(1024)}, u32[]{:S(2)}) copy-start(f32[1024]{0:T(1024)} %param.14) | copy-start | bytes 12292
Sparse Core Ops, SparseCore 0:
  8.9 108.6 all-gather.5
  294.1 481.8 all-gather.3
where the time goes:
time: 826 us; the launch traced here: 816 us
  waiting for transfers between devices  483 us (58%)
  matrix products  146 us (18%)
  local copies, waits for them, and re-layouts  97.3 us (12%)
  other arithmetic  65.8 us (8%)
  between operations  14.1 us (2%)
    all_gather x1, waiting for transfers between devices, on_device(): lax.all_gather(gated_out, 'chan', axis=1, tiled=True)  482 us
    dot_general x1, matrix products, on_device(): within = jnp.einsum('tsc,bsc->btc', toeplitz, blocks, precision=HIGHEST)  58.4 us
    gather x2, local copies, waits for them, and re-layouts, on_device(): jnp.take(kernel, jnp.maximum(lag_matrix, 0), axis=0)  49 us
    dot_general x1, matrix products, on_device(): jnp.dot(lax.all_gather(gated_out, 'chan', axis=1, tiled=True), weight_col...  33 us
    dot_general x1, matrix products, on_device(): across = jnp.einsum('tcn,bcn->btc', lead_decay, state_in, precision=HIGHEST)  29.6 us
    dot_general x1, matrix products, on_device(): jnp.einsum('bsc,scn->bcn', blocks, tail_decay, precision=HIGHEST)  24.5 us
  transfers between devices with their start and end apart: 3, of which 2 were waited for; matrix products, arithmetic and copies ran while one was open for 34% of the time, Pallas kernels for 0%

commit v1 on v0

v1 whole, which is shorter than its diff:
```python
import functools

import jax
import jax.numpy as jnp
from jax import lax
from jax.experimental import pallas as pl
from jax.experimental.pallas import tpu as pltpu
from jax.sharding import PartitionSpec as P

MESH = pl.DeviceIdType.MESH
SEGMENTS = 8
LANES = 128
HALO = 8
PIECES = 4
MIB = 1024 * 1024


def short_stream(x_ref, edge_ref, taps, padded, result_of, length):
    padded[HALO - edge_ref.shape[0] : HALO, :] = edge_ref[...].astype(jnp.float32)
    for seg in range(SEGMENTS):
        at = seg * length
        padded[HALO + at : HALO + at + length, :] = x_ref[at : at + length, :].astype(jnp.float32)
    for seg in range(SEGMENTS):
        at = seg * length
        total = None
        for tap in range(taps.shape[0]):
            begin = HALO + at - tap
            term = taps[tap : tap + 1, :] * padded[begin : begin + length, :]
            total = term if total is None else total + term
        result_of(at, total)


def write_to(ref, length):
    def put(at, value):
        ref[at : at + length, :] = value

    return put


def multiply_into(ref, length):
    def put(at, value):
        ref[at : at + length, :] = ref[at : at + length, :] * value

    return put


def ends_kernel(k_ref, v_ref, edge_ref, taps_ref, rate_ref, seg_ref, end_ref, padded, drive):
    tokens = k_ref.shape[0]
    modes = rate_ref.shape[0]
    length = tokens // SEGMENTS
    short_stream(k_ref, edge_ref.at[1], taps_ref.at[1], padded, write_to(drive, length), length)
    short_stream(v_ref, edge_ref.at[2], taps_ref.at[2], padded, multiply_into(drive, length), length)
    decay = jnp.exp(-rate_ref[...])
    decays = [jnp.broadcast_to(decay[n : n + 1, :], (SEGMENTS, LANES)) for n in range(modes)]
    unroll = 4

    def steps(block, states):
        for inner in range(unroll):
            u = drive[pl.ds(block * unroll + inner, SEGMENTS, stride=length), :]
            states = tuple(decays[n] * states[n] + u for n in range(modes))
        return states

    zero = jnp.zeros((SEGMENTS, LANES), jnp.float32)
    states = lax.fori_loop(0, length // unroll, steps, (zero,) * modes)
    for n in range(modes):
        seg_ref[n] = states[n]
    span = jnp.exp(-rate_ref[...] * float(length))
    total = jnp.zeros((modes, LANES), jnp.float32)
    for seg in range(SEGMENTS):
        total = span * total + seg_ref[:, seg, :]
    end_ref[...] = total


def gated_kernel(
    q_ref, k_ref, v_ref, edge_ref, taps_ref, rate_ref, gain_ref, skip_ref, seg_ref, carry_ref,
    out_ref, padded, drive, query, conv, starts,
):
    tokens = k_ref.shape[0]
    modes = rate_ref.shape[0]
    length = tokens // SEGMENTS
    short_stream(q_ref, edge_ref.at[0], taps_ref.at[0], padded, write_to(query, length), length)
    short_stream(k_ref, edge_ref.at[1], taps_ref.at[1], padded, write_to(drive, length), length)
    short_stream(v_ref, edge_ref.at[2], taps_ref.at[2], padded, multiply_into(drive, length), length)
    span = jnp.exp(-rate_ref[...] * float(length))
    state = carry_ref[...]
    for seg in range(SEGMENTS):
        starts[:, seg, :] = state
        state = span * state + seg_ref[:, seg, :]
    decay = jnp.exp(-rate_ref[...])
    gain = gain_ref[...]
    decays = [jnp.broadcast_to(decay[n : n + 1, :], (SEGMENTS, LANES)) for n in range(modes)]
    gains = [jnp.broadcast_to(gain[n : n + 1, :], (SEGMENTS, LANES)) for n in range(modes)]
    unroll = 4

    def steps(block, states):
        for inner in range(unroll):
            at = block * unroll + inner
            u = drive[pl.ds(at, SEGMENTS, stride=length), :]
            states = tuple(decays[n] * states[n] + u for n in range(modes))
            even, odd = gains[0] * states[0], gains[1] * states[1]
            for n in range(2, modes, 2):
                even = even + gains[n] * states[n]
                odd = odd + gains[n + 1] * states[n + 1]
            conv[pl.ds(at, SEGMENTS, stride=length), :] = even + odd
        return states

    lax.fori_loop(0, length // unroll, steps, tuple(starts[n] for n in range(modes)))
    for seg in range(SEGMENTS):
        at = seg * length
        rows = slice(at, at + length)
        out_ref[rows, :] = (
            query[rows, :] * (conv[rows, :] + skip_ref[...] * drive[rows, :])
        ).astype(out_ref.dtype)


def route(shards):
    line = shards // 2
    plans = []
    for me in range(shards):
        z, y = me // 2, me % 2
        events = []
        for shard in range(shards):
            from_z, from_y = shard // 2, shard % 2
            apart = abs(from_z - z)
            halves = []
            for half in range(2):
                if from_y == y:
                    low = z > 0 and from_z >= z
                    high = z < line - 1 and from_z <= z
                    pair = not (half == 1 and apart == 1)
                    key = float(apart)
                else:
                    low = z > 0 and apart == 0 and half == 1
                    high = z < line - 1 and apart == 0 and half == 1
                    pair = False
                    key = apart + 0.5
                halves.append((low, high, pair))
            events.append((key, shard, halves))
        events.sort(key=lambda e: (e[0], e[1]))
        plans.append([
            (shard, [int(a) + 2 * int(b) + 4 * int(c) for a, b, c in halves])
            for _, shard, halves in events
        ])
    return plans


def pick(values, index):
    result = jnp.int32(values[0])
    for position in range(1, len(values)):
        result = jnp.where(index == position, values[position], result)
    return result


def mix_kernel(shards, blocks, g_ref, w_ref, out_ref, held, weight, total, own_sem, wown_sem, send_sem, recv_sem, wsend_sem, wrecv_sem):
    tokens, width = g_ref.shape
    depth, columns = w_ref.shape
    rows = tokens // PIECES
    me = lax.axis_index("chan")
    ctx = lax.axis_index("ctx")
    line = shards // 2
    z, y = me // 2, me % 2
    plans = route(shards)
    codes = [
        pick([plan[k][0] + shards * (plan[k][1][0] + 8 * plan[k][1][1]) for plan in plans], me)
        for k in range(shards)
    ]
    targets = (me - 2, me + 2, me + 1 - 2 * y)

    def flip(by):
        result, bit = ctx, 1
        while bit <= by:
            if by & bit:
                result = result + bit * (1 - 2 * ((ctx // bit) % 2))
            bit *= 2
        return result

    def block_of(index):
        return weight.at[pl.ds(pl.multiple_of(index * depth, depth), depth), :]

    own_copy = pltpu.make_async_copy(g_ref, held.at[me], own_sem)
    own_copy.start()
    weight_copy = pltpu.make_async_copy(w_ref, block_of(ctx), wown_sem)
    weight_copy.start()

    barrier = pltpu.get_barrier_semaphore()

    @pl.when(z > 0)
    def _():
        pl.semaphore_signal(barrier, inc=1, device_id={"chan": targets[0]}, device_id_type=MESH)

    @pl.when(z < line - 1)
    def _():
        pl.semaphore_signal(barrier, inc=1, device_id={"chan": targets[1]}, device_id_type=MESH)

    pl.semaphore_signal(barrier, inc=1, device_id={"chan": targets[2]}, device_id_type=MESH)
    partners = [1] + list(range(2, blocks, 2))
    for by in partners:
        pl.semaphore_signal(barrier, inc=1, device_id={"ctx": flip(by)}, device_id_type=MESH)
    lines = jnp.where(z > 0, 1, 0) + jnp.where(z < line - 1, 1, 0)
    pl.semaphore_wait(barrier, lines + 1 + len(partners))

    def piece_copy(shard, piece, way):
        part = held.at[shard, pl.ds(pl.multiple_of(piece * rows, rows), rows), :]
        return pltpu.make_async_remote_copy(
            src_ref=part,
            dst_ref=part,
            send_sem=send_sem.at[shard, piece, way],
            recv_sem=recv_sem.at[shard, piece],
            device_id={"chan": targets[way]},
            device_id_type=MESH,
        )

    def weight_send(block, by, slot):
        return pltpu.make_async_remote_copy(
            src_ref=block_of(block),
            dst_ref=block_of(block),
            send_sem=wsend_sem.at[slot],
            recv_sem=wrecv_sem.at[block],
            device_id={"ctx": flip(by)},
            device_id_type=MESH,
        )

    def onward(code, piece, act):
        shard = code % shards
        flags = code // shards
        flags = jnp.where(piece < PIECES // 2, flags % 8, flags // 8)
        for way, bit in ((0, flags % 2), (1, (flags // 2) % 2), (2, flags // 4)):

            @pl.when(bit == 1)
            def _(way=way):
                act(piece_copy(shard, piece, way))

    own_copy.wait()

    @pl.loop(0, PIECES)
    def _(piece):
        onward(codes[0], piece, lambda copy: copy.start())

    weight_copy.wait()
    first_sends = [weight_send(ctx, by, slot) for slot, by in enumerate(partners)]
    for copy in first_sends:
        copy.start()

    def zero_rows(at):
        total[pl.ds(pl.multiple_of(at * 64, 64), 64), :] = jnp.zeros((64, columns), jnp.float32)

    pl.loop(0, tokens // 64)(zero_rows)

    def arrive(code, piece):
        piece_copy(code % shards, piece, 2).wait_recv()
        onward(code, piece, lambda copy: copy.start())

    half = shards // 2
    later_sends = []
    for k in range(1, half):
        code = codes[k]
        if k < half - 1:

            @pl.loop(0, PIECES)
            def _(piece, code=code):
                arrive(code, piece)
        else:

            @pl.loop(0, PIECES // 2)
            def _(piece, code=code):
                arrive(code, piece)

            for by in partners[1:]:
                block = flip(by)
                weight_send(block, 1, 0).wait_recv()
                copy = weight_send(block, 1, len(partners) + len(later_sends))
                copy.start()
                later_sends.append(copy)

            @pl.loop(PIECES // 2, PIECES)
            def _(piece, code=code):
                arrive(code, piece)

    weight_send(flip(1), 1, 0).wait_recv()
    for by in partners[1:]:
        weight_send(flip(by + 1), 1, 0).wait_recv()

    tile = 256

    def multiply(shard, piece):
        here = pl.ds(pl.multiple_of(piece * rows, rows), rows)
        deep = pl.ds(pl.multiple_of(shard * width, width), width)

        @pl.loop(0, columns // tile)
        def _(part):
            cols = pl.ds(pl.multiple_of(part * tile, tile), tile)
            total[here, cols] += jnp.dot(
                held[shard, here, :], weight[deep, cols], preferred_element_type=jnp.float32
            )

    @pl.loop(half, shards)
    def _(k):
        code = pick(codes, k)
        earlier = pick(codes, 2 * (k - half)) % shards
        later = pick(codes, 2 * (k - half) + 1) % shards

        @pl.loop(0, PIECES)
        def _(piece):
            arrive(code, piece)
            multiply(earlier, piece)
            multiply(later, piece)

    def round_rows(at):
        here = pl.ds(pl.multiple_of(at * 64, 64), 64)
        out_ref[here, :] = total[here, :].astype(out_ref.dtype)

    pl.loop(0, tokens // 64)(round_rows)

    @pl.loop(0, shards)
    def _(k):
        code = pick(codes, k)

        @pl.loop(0, PIECES)
        def _(piece):
            onward(code, piece, lambda copy: copy.wait_send())

    for copy in first_sends + later_sends:
        copy.wait_send()


def on_device(query_in, key_in, value_in, short_filter, residue, decay_rate, skip_gain, out_weight):
    tokens, channels = query_in.shape
    tap_count = short_filter.shape[1]
    modes = decay_rate.shape[1]
    shards = lax.axis_size("chan")
    blocks = lax.axis_size("ctx")
    position = lax.axis_index("ctx")
    edge = jnp.stack([x[tokens - (tap_count - 1) :, :] for x in (query_in, key_in, value_in)])
    edge = lax.ppermute(edge, "ctx", [(i, i + 1) for i in range(blocks - 1)])
    rate = decay_rate.T
    gain = (residue * jnp.sqrt(decay_rate)).T
    skip = skip_gain[None, :]

    stream = pl.BlockSpec((tokens, LANES), lambda i: (0, i))
    edges = pl.BlockSpec((3, tap_count - 1, LANES), lambda i: (0, 0, i))
    taps = pl.BlockSpec((3, tap_count, LANES), lambda i: (0, 0, i))
    mode = pl.BlockSpec((modes, LANES), lambda i: (0, i))
    segs = pl.BlockSpec((modes, SEGMENTS, LANES), lambda i: (0, 0, i))
    flat = pltpu.VMEM((tokens, LANES), jnp.float32)
    pad = pltpu.VMEM((tokens + HALO, LANES), jnp.float32)
    chunks = channels // LANES
    work = tokens * channels * modes

    segment_ends, local_end = pl.pallas_call(
        ends_kernel,
        grid=(chunks,),
        in_specs=[stream, stream, edges, taps, mode],
        out_specs=[segs, mode],
        out_shape=[
            jax.ShapeDtypeStruct((modes, SEGMENTS, channels), jnp.float32),
            jax.ShapeDtypeStruct((modes, channels), jnp.float32),
        ],
        scratch_shapes=[pad, flat],
        compiler_params=pltpu.CompilerParams(vmem_limit_bytes=32 * MIB),
        cost_estimate=pl.CostEstimate(flops=2 * work, bytes_accessed=4 * tokens * channels, transcendentals=0),
        name="segment_ends",
    )(key_in, value_in, edge, short_filter, rate)

    ends = lax.all_gather(local_end[None], "ctx", axis=0, tiled=True)
    hops = position - 1 - jnp.arange(blocks)
    span = (tokens * jnp.maximum(hops, 0)).astype(jnp.float32)
    weights = jnp.where(
        (hops >= 0)[:, None, None], jnp.exp(-rate[None] * span[:, None, None]), 0.0
    )
    carry = jnp.sum(weights * ends, axis=0)

    gated = pl.pallas_call(
        gated_kernel,
        grid=(chunks,),
        in_specs=[
            stream, stream, stream, edges, taps, mode, mode,
            pl.BlockSpec((1, LANES), lambda i: (0, i)), segs, mode,
        ],
        out_specs=stream,
        out_shape=jax.ShapeDtypeStruct((tokens, channels), jnp.bfloat16),
        scratch_shapes=[pad, flat, flat, flat, pltpu.VMEM((modes, SEGMENTS, LANES), jnp.float32)],
        compiler_params=pltpu.CompilerParams(vmem_limit_bytes=32 * MIB),
        cost_estimate=pl.CostEstimate(flops=4 * work, bytes_accessed=8 * tokens * channels, transcendentals=0),
        name="gated",
    )(query_in, key_in, value_in, edge, short_filter, rate, gain, skip, segment_ends, carry)

    depth, columns = out_weight.shape
    partners = blocks // 2
    return pl.pallas_call(
        functools.partial(mix_kernel, shards, blocks),
        in_specs=[pl.BlockSpec(memory_space=pl.ANY)] * 2,
        out_specs=pl.BlockSpec(memory_space=pltpu.VMEM),
        out_shape=jax.ShapeDtypeStruct((tokens, columns), jnp.bfloat16),
        scratch_shapes=[
            pltpu.VMEM((shards, tokens, channels), jnp.bfloat16),
            pltpu.VMEM((blocks * depth, columns), jnp.bfloat16),
            pltpu.VMEM((tokens, columns), jnp.float32),
            pltpu.SemaphoreType.DMA,
            pltpu.SemaphoreType.DMA,
            pltpu.SemaphoreType.DMA((shards, PIECES, 3)),
            pltpu.SemaphoreType.DMA((shards, PIECES)),
            pltpu.SemaphoreType.DMA((2 * partners,)),
            pltpu.SemaphoreType.DMA((blocks,)),
        ],
        compiler_params=pltpu.CompilerParams(
            collective_id=0, has_side_effects=True, vmem_limit_bytes=60 * MIB
        ),
        cost_estimate=pl.CostEstimate(
            flops=2 * tokens * shards * channels * columns,
            bytes_accessed=2 * tokens * channels + 2 * depth * columns + 2 * tokens * columns,
            transcendentals=0,
        ),
        name="mix",
    )(gated, out_weight)


def solution(mesh):
    in_specs = (
        P("ctx", "chan"),
        P("ctx", "chan"),
        P("ctx", "chan"),
        P(None, None, "chan"),
        P("chan", None),
        P("chan", None),
        P("chan"),
        P("ctx", "chan"),
    )
    return jax.shard_map(
        on_device, mesh=mesh, in_specs=in_specs, out_specs=P("ctx", "chan"), check_vma=False
    )
```

time: 826 us -> 341 us (0.41); the launches traced: 816 us -> 341 us
  waiting for transfers between devices: 483 us -> 0.01 us
  Pallas kernels: 0 us -> 316 us
  matrix products: 146 us -> 0 us
  local copies, waits for them, and re-layouts: 97.3 us -> 12.4 us
  other arithmetic: 65.8 us -> 1.9 us
  between operations: 14.1 us -> 0.12 us
    all_gather x2 -> x0, waiting for transfers between devices: 482 us -> none  [the longest x1 482 us: on_device(): lax.all_gather(gated_out, 'chan', axis=1, tiled=True)]
    pallas_call x0 -> x3, Pallas kernels: none -> 316 us  [the longest x1 270 us: on_device(): pl.pallas_call(functools.partial(mix_kernel, shards, blocks), in_specs=[p...]
    dot_general x4 -> x0, matrix products: 146 us -> none  [the longest x1 58.4 us: on_device(): within = jnp.einsum('tsc,bsc->btc', toeplitz, blocks, precision=HIGHEST)]
    gather x2 -> x0, local copies, waits for them, and re-layouts: 49 us -> none  [on_device(): jnp.take(kernel, jnp.maximum(lag_matrix, 0), axis=0)]
    convert_element_type x5 -> x1, other arithmetic: 18 us -> 0.01 us  [on_device(): span = (tokens * jnp.maximum(hops, 0)).astype(jnp.float32)]
    add x2 -> x0, local copies, waits for them, and re-layouts: 16.4 us -> none  [the longest x1 9.79 us: on_device(): mode_conv = (within + across).reshape(tokens, channels)]
    slice x3 -> x0, local copies, waits for them, and re-layouts: 14.2 us -> none  [the longest x2 14.2 us: on_device(): local_end = jnp.exp(-decay_rate * block_len) * prefix[-1] + block_ends[-1]]
    add x4 -> x0, other arithmetic: 13.5 us -> none  [the longest x1 11.7 us: short_pass(): result + short_filter[:, tap_index, None, :] * padded[:, begin:begin + le...]
  transfers between devices with their start and end apart: 3 -> 1, of which waited for: 2 -> 0; matrix products, arithmetic and copies ran while one was open for 34% -> 1% of each run, Pallas kernels for 0% -> 0%
where the time goes in v1:
time: 341 us
  Pallas kernels  316 us (93%)
  local copies, waits for them, and re-layouts  12.4 us (4%)
  blocking collectives  8.12 us (2%)
    pallas_call x1, Pallas kernels, on_device(): pl.pallas_call(functools.partial(mix_kernel, shards, blocks), in_specs=[p...  270 us
    pallas_call x1, Pallas kernels, on_device(): pl.pallas_call(gated_kernel, grid=(chunks,), in_specs=[stream, stream, st...  29.4 us
    pallas_call x1, Pallas kernels, on_device(): pl.pallas_call(ends_kernel, grid=(chunks,), in_specs=[stream, stream, edg...  16 us
    unnamed x15, local copies, waits for them, and re-layouts  10.9 us
    all_gather x1, blocking collectives, on_device(): ends = lax.all_gather(local_end[None], 'ctx', axis=0, tiled=True)  8.12 us
  transfers between devices with their start and end apart: 1, of which 0 were waited for; matrix products, arithmetic and copies ran while one was open for 1% of the time, Pallas kernels for 0%

profile of v1, /device:TPU:0, one launch (start us, length us, event | category | flops | bytes accessed | tf_op | source)
XLA Modules:
  0.0 340.7 jit_solution(9928966847248928544)
XLA Ops:
  0.0 0.7 slice_bitcast_fusion.2
  0.7 0.7 slice_bitcast_fusion
  1.5 2.4 collective-permute-start
  3.9 0.8 bitcast_negate_fusion
  4.7 0.9 multiply_bitcast_fusion.gain_ref
  5.6 0.0 collective-permute-done.edge_ref
  5.7 0.0 copy-start
  5.7 1.9 copy-done
  7.6 0.0 copy-start.1
  7.6 1.9 copy-done.1
  9.4 0.0 copy-start.4
  9.4 0.8 copy-done.4
  10.3 0.0 copy-start.5
  10.3 0.8 copy-done.5
  11.1 0.0 copy-start.2
  11.1 0.0 copy-start.6
  11.1 16.0 %segment_ends.1 = (f32[16,8,1024]{2,1,0:T(8,128)S(1)}, f32[16,1024]{1,0:T(8,128)S(1)}) custom-call(bf16[1536,1024]{1,0:T(8,128)(2,1)S(1)} %copy-done, bf16[1536,1024]{1,0:T(8,128)(2,1)S(1)} %copy-done.1, bf16[3,2,1024]{2,1,0:T(2,128)(2,1)S(1)} %collective-permute-done.edge_ref, f32[3,3,1024]{2,1,0:T(4,128)S(1)} %copy-done.5, f32[16,1024]{1,0:T(8,128)S(1)} %bitcast.12), custom_call_target="tpu_custom_call" | custom-call | flops 50331648 | bytes 6291456 | tf_op jit(solution)/shard_map/segment_ends/pallas_call | solution.py:349
  27.1 8.1 %all-gather = f32[64,1024]{1,0:T(8,128)S(1)} all-gather(f32[16,1024]{1,0:T(8,128)S(1)} %get-tuple-element.8), channel_id=2, replica_groups=mesh['chan'=8,'ctx'=4] {'ctx'}, dimensions={0}, use_global_device_ids=true | all-gather | bytes 327680 | tf_op jit(solution)/shard_map/all_gather | solution.py:364
  35.3 0.1 multiply_reduce_fusion.carry_ref
  35.4 0.0 copy-done.2
  35.4 0.0 copy-done.6
  35.4 29.4 %gated.1.g_ref = bf16[1536,1024]{1,0:T(8,128)(2,1)S(1)} custom-call(bf16[1536,1024]{1,0:T(8,128)(2,1)S(1)} %copy-done.2, bf16[1536,1024]{1,0:T(8,128)(2,1)S(1)} %copy-done, bf16[1536,1024]{1,0:T(8,128)(2,1)S(1)} %copy-done.1, bf16[3,2,1024]{2,1,0:T(2,128)(2,1)S(1)} %collective-permute-done.edge_ref, f32[3,3,1024]{2,1,0:T(4,128)S(1)} %copy-done.5, ...), custom_call_target="tpu_custom_call" | custom-call | flops 100663296 | bytes 12582912 | tf_op jit(solution)/shard_map/gated/pallas_call | solution.py:372
  64.8 0.0 copy-start.3
  64.9 1.7 copy-done.3
  66.5 270.3 %mix.1 = bf16[1536,1024]{1,0:T(8,128)(2,1)} custom-call(bf16[1536,1024]{1,0:T(8,128)(2,1)} %copy-done.3, bf16[2048,1024]{1,0:T(8,128)(2,1)} %w_ref.1), custom_call_target="tpu_custom_call" | custom-call | flops 25769803776 | bytes 10485760 | tf_op jit(solution)/shard_map/mix/pallas_call | solution.py:389
  336.8 3.9 %copy.10 = bf16[1536,1024]{1,0:T(8,128)(2,1)} copy(bf16[1536,1024]{1,0:T(8,128)(2,1)} %mix.1) | data formatting | bytes 6291456
  (3 shorter events, 0.0 us)
Async XLA Ops:
  1.5 4.1 %collective-permute-start = (bf16[3,2,1024]{2,1,0:T(2,128)(2,1)S(1)}, bf16[3,2,1024]{2,1,0:T(2,128)(2,1)S(1)}, u32[]{:S(2)}, u32[]{:S(2)}) collective-permute-start(bf16[3,2,1024]{2,1,0:T(2,128)(2,1)S(1)} %pad_maximum_fusion), channel_id=1, source_target_pairs={{0,1},{1,2},{2,3},{4,5},{5,6},{6,7},{8,9},{9,10},{10,11},{12,13},{... | collective-permute-start | bytes 36872 | tf_op jit(solution)/shard_map/ppermute | solution.py:334
  5.7 1.9 copy-start
  7.6 1.9 copy-start.1
  9.4 0.8 copy-start.4
  10.3 0.8 copy-start.5
  11.1 24.3 %copy-start.2 = (bf16[1536,1024]{1,0:T(8,128)(2,1)S(1)}, bf16[1536,1024]{1,0:T(8,128)(2,1)}, u32[]{:S(2)}) copy-start(bf16[1536,1024]{1,0:T(8,128)(2,1)} %q_ref.1) | copy-start | bytes 9437188
  11.1 24.3 %copy-start.6 = (f32[1024]{0:T(1024)S(1)}, f32[1024]{0:T(1024)}, u32[]{:S(2)}) copy-start(f32[1024]{0:T(1024)} %param.14) | copy-start | bytes 12292
  64.8 1.7 copy-start.3

commit v2 on v1

--- a/solution.py
+++ b/solution.py
@@ -16,7 +16,7 @@
 
 
 def short_stream(x_ref, edge_ref, taps, padded, result_of, length):
-    padded[HALO - edge_ref.shape[0] : HALO, :] = edge_ref[...].astype(jnp.float32)
+    padded[HALO - edge_ref.shape[0] : HALO, :] = edge_ref[...]
     for seg in range(SEGMENTS):
         at = seg * length
         padded[HALO + at : HALO + at + length, :] = x_ref[at : at + length, :].astype(jnp.float32)
@@ -71,23 +71,23 @@
     end_ref[...] = total
 
 
-def gated_kernel(
-    q_ref, k_ref, v_ref, edge_ref, taps_ref, rate_ref, gain_ref, skip_ref, seg_ref, carry_ref,
+def gate_chunk(
+    streams, edge_ref, taps_ref, rate, gain, skip, seg_ref, carry,
     out_ref, padded, drive, query, conv, starts,
 ):
-    tokens = k_ref.shape[0]
-    modes = rate_ref.shape[0]
+    tokens = drive.shape[0]
+    modes = rate.shape[0]
     length = tokens // SEGMENTS
+    q_ref, k_ref, v_ref = streams
     short_stream(q_ref, edge_ref.at[0], taps_ref.at[0], padded, write_to(query, length), length)
     short_stream(k_ref, edge_ref.at[1], taps_ref.at[1], padded, write_to(drive, length), length)
     short_stream(v_ref, edge_ref.at[2], taps_ref.at[2], padded, multiply_into(drive, length), length)
-    span = jnp.exp(-rate_ref[...] * float(length))
-    state = carry_ref[...]
+    span = jnp.exp(-rate * float(length))
+    state = carry
     for seg in range(SEGMENTS):
         starts[:, seg, :] = state
         state = span * state + seg_ref[:, seg, :]
-    decay = jnp.exp(-rate_ref[...])
-    gain = gain_ref[...]
+    decay = jnp.exp(-rate)
     decays = [jnp.broadcast_to(decay[n : n + 1, :], (SEGMENTS, LANES)) for n in range(modes)]
     gains = [jnp.broadcast_to(gain[n : n + 1, :], (SEGMENTS, LANES)) for n in range(modes)]
     unroll = 4
@@ -109,7 +109,7 @@
         at = seg * length
         rows = slice(at, at + length)
         out_ref[rows, :] = (
-            query[rows, :] * (conv[rows, :] + skip_ref[...] * drive[rows, :])
+            query[rows, :] * (conv[rows, :] + skip * drive[rows, :])
         ).astype(out_ref.dtype)
 
 
@@ -151,10 +151,16 @@
     return result
 
 
-def mix_kernel(shards, blocks, g_ref, w_ref, out_ref, held, weight, total, own_sem, wown_sem, send_sem, recv_sem, wsend_sem, wrecv_sem):
-    tokens, width = g_ref.shape
+def mix_kernel(
+    shards, blocks, q_ref, k_ref, v_ref, w_ref, edge_ref, taps_ref, rate_ref, gain_ref, skip_ref,
+    seg_ref, carry_ref, out_ref, held, weight, total, streams, padded, drive, query, conv, starts,
+    in_sem, wown_sem, send_sem, recv_sem, wsend_sem, wrecv_sem,
+):
+    tokens, channels = q_ref.shape
     depth, columns = w_ref.shape
-    rows = tokens // PIECES
+    width = channels // PIECES
+    chunks = channels // LANES
+    per_piece = width // LANES
     me = lax.axis_index("chan")
     ctx = lax.axis_index("ctx")
     line = shards // 2
@@ -177,8 +183,17 @@
     def block_of(index):
         return weight.at[pl.ds(pl.multiple_of(index * depth, depth), depth), :]
 
-    own_copy = pltpu.make_async_copy(g_ref, held.at[me], own_sem)
-    own_copy.start()
+    def fetch(chunk, act):
+        slot = chunk % 2
+        lanes = pl.ds(pl.multiple_of(chunk * LANES, LANES), LANES)
+        for which, ref in enumerate((q_ref, k_ref, v_ref)):
+            act(
+                pltpu.make_async_copy(
+                    ref.at[:, lanes], streams.at[slot, which], in_sem.at[slot, which]
+                )
+            )
+
+    fetch(0, lambda copy: copy.start())
     weight_copy = pltpu.make_async_copy(w_ref, block_of(ctx), wown_sem)
     weight_copy.start()
 
@@ -200,7 +215,7 @@
     pl.semaphore_wait(barrier, lines + 1 + len(partners))
 
     def piece_copy(shard, piece, way):
-        part = held.at[shard, pl.ds(pl.multiple_of(piece * rows, rows), rows), :]
+        part = held.at[shard, piece]
         return pltpu.make_async_remote_copy(
             src_ref=part,
             dst_ref=part,
@@ -230,16 +245,37 @@
             def _(way=way):
                 act(piece_copy(shard, piece, way))
 
-    own_copy.wait()
-
-    @pl.loop(0, PIECES)
-    def _(piece):
-        onward(codes[0], piece, lambda copy: copy.start())
-
     weight_copy.wait()
     first_sends = [weight_send(ctx, by, slot) for slot, by in enumerate(partners)]
     for copy in first_sends:
         copy.start()
+
+    @pl.loop(0, chunks)
+    def _(chunk):
+        @pl.when(chunk < chunks - 1)
+        def _():
+            fetch(chunk + 1, lambda copy: copy.start())
+
+        fetch(chunk, lambda copy: copy.wait())
+        piece = chunk // per_piece
+        lanes = pl.ds(pl.multiple_of(chunk * LANES, LANES), LANES)
+        inside = pl.ds(pl.multiple_of((chunk % per_piece) * LANES, LANES), LANES)
+        gate_chunk(
+            [streams.at[chunk % 2, which] for which in range(3)],
+            edge_ref.at[:, :, lanes],
+            taps_ref.at[:, :, lanes],
+            rate_ref[:, lanes],
+            gain_ref[:, lanes],
+            skip_ref[:, lanes],
+            seg_ref.at[:, :, lanes],
+            carry_ref[:, lanes],
+            held.at[me, piece, :, inside],
+            padded, drive, query, conv, starts,
+        )
+
+        @pl.when(chunk % per_piece == per_piece - 1)
+        def _():
+            onward(codes[0], piece, lambda copy: copy.start())
 
     def zero_rows(at):
         total[pl.ds(pl.multiple_of(at * 64, 64), 64), :] = jnp.zeros((64, columns), jnp.float32)
@@ -282,16 +318,20 @@
 
     tile = 256
 
+    rows = tokens // 2
+
     def multiply(shard, piece):
-        here = pl.ds(pl.multiple_of(piece * rows, rows), rows)
-        deep = pl.ds(pl.multiple_of(shard * width, width), width)
+        deep = pl.ds(pl.multiple_of(shard * channels + piece * width, width), width)
 
         @pl.loop(0, columns // tile)
         def _(part):
             cols = pl.ds(pl.multiple_of(part * tile, tile), tile)
-            total[here, cols] += jnp.dot(
-                held[shard, here, :], weight[deep, cols], preferred_element_type=jnp.float32
-            )
+            for at in range(0, tokens, rows):
+                total[at : at + rows, cols] += jnp.dot(
+                    held[shard, piece, at : at + rows, :],
+                    weight[deep, cols],
+                    preferred_element_type=jnp.float32,
+                )
 
     @pl.loop(half, shards)
     def _(k):
@@ -332,6 +372,7 @@
     position = lax.axis_index("ctx")
     edge = jnp.stack([x[tokens - (tap_count - 1) :, :] for x in (query_in, key_in, value_in)])
     edge = lax.ppermute(edge, "ctx", [(i, i + 1) for i in range(blocks - 1)])
+    edge = edge.astype(jnp.float32)
     rate = decay_rate.T
     gain = (residue * jnp.sqrt(decay_rate)).T
     skip = skip_gain[None, :]
@@ -369,33 +410,25 @@
     )
     carry = jnp.sum(weights * ends, axis=0)
 
-    gated = pl.pallas_call(
-        gated_kernel,
-        grid=(chunks,),
-        in_specs=[
-            stream, stream, stream, edges, taps, mode, mode,
-            pl.BlockSpec((1, LANES), lambda i: (0, i)), segs, mode,
-        ],
-        out_specs=stream,
-        out_shape=jax.ShapeDtypeStruct((tokens, channels), jnp.bfloat16),
-        scratch_shapes=[pad, flat, flat, flat, pltpu.VMEM((modes, SEGMENTS, LANES), jnp.float32)],
-        compiler_params=pltpu.CompilerParams(vmem_limit_bytes=32 * MIB),
-        cost_estimate=pl.CostEstimate(flops=4 * work, bytes_accessed=8 * tokens * channels, transcendentals=0),
-        name="gated",
-    )(query_in, key_in, value_in, edge, short_filter, rate, gain, skip, segment_ends, carry)
-
     depth, columns = out_weight.shape
     partners = blocks // 2
     return pl.pallas_call(
         functools.partial(mix_kernel, shards, blocks),
-        in_specs=[pl.BlockSpec(memory_space=pl.ANY)] * 2,
+        in_specs=[pl.BlockSpec(memory_space=pl.ANY)] * 4
+        + [pl.BlockSpec(memory_space=pltpu.VMEM)] * 7,
         out_specs=pl.BlockSpec(memory_space=pltpu.VMEM),
         out_shape=jax.ShapeDtypeStruct((tokens, columns), jnp.bfloat16),
         scratch_shapes=[
-            pltpu.VMEM((shards, tokens, channels), jnp.bfloat16),
+            pltpu.VMEM((shards, PIECES, tokens, channels // PIECES), jnp.bfloat16),
             pltpu.VMEM((blocks * depth, columns), jnp.bfloat16),
             pltpu.VMEM((tokens, columns), jnp.float32),
-            pltpu.SemaphoreType.DMA,
+            pltpu.VMEM((2, 3, tokens, LANES), jnp.bfloat16),
+            pad,
+            flat,
+            flat,
+            flat,
+            pltpu.VMEM((modes, SEGMENTS, LANES), jnp.float32),
+            pltpu.SemaphoreType.DMA((2, 3)),
             pltpu.SemaphoreType.DMA,
             pltpu.SemaphoreType.DMA((shards, PIECES, 3)),
             pltpu.SemaphoreType.DMA((shards, PIECES)),
@@ -403,15 +436,18 @@
             pltpu.SemaphoreType.DMA((blocks,)),
         ],
         compiler_params=pltpu.CompilerParams(
-            collective_id=0, has_side_effects=True, vmem_limit_bytes=60 * MIB
+            collective_id=0, has_side_effects=True, vmem_limit_bytes=62 * MIB
         ),
         cost_estimate=pl.CostEstimate(
-            flops=2 * tokens * shards * channels * columns,
-            bytes_accessed=2 * tokens * channels + 2 * depth * columns + 2 * tokens * columns,
+            flops=2 * tokens * shards * channels * columns + 4 * work,
+            bytes_accessed=6 * tokens * channels + 2 * depth * columns + 2 * tokens * columns,
             transcendentals=0,
         ),
         name="mix",
-    )(gated, out_weight)
+    )(
+        query_in, key_in, value_in, out_weight, edge, short_filter, rate, gain, skip,
+        segment_ends, carry,
+    )
 
 
 def solution(mesh):

time: 341 us -> 320 us (0.938)
  Pallas kernels: 316 us -> 295 us
    pallas_call x1 -> x0, Pallas kernels: 29.4 us -> none  [on_device(): pl.pallas_call(gated_kernel, grid=(chunks,), in_specs=[stream, stream, st...]
    pallas_call x1, Pallas kernels: 270 us -> 279 us  [on_device(): pl.pallas_call(functools.partial(mix_kernel, shards, blocks), in_specs=[p...]
    unnamed x15 -> x13, local copies, waits for them, and re-layouts: 10.9 us -> 10.1 us
where the time goes in v2:
time: 320 us; the launch traced here: 319 us
  Pallas kernels  295 us (92%)
  local copies, waits for them, and re-layouts  11.5 us (4%)
  blocking collectives  7.29 us (2%)
    pallas_call x1, Pallas kernels, on_device(): pl.pallas_call(functools.partial(mix_kernel, shards, blocks), in_specs=[p...  279 us
    pallas_call x1, Pallas kernels, on_device(): pl.pallas_call(ends_kernel, grid=(chunks,), in_specs=[stream, stream, edg...  16.1 us
    unnamed x13, local copies, waits for them, and re-layouts  10.1 us
    all_gather x1, blocking collectives, on_device(): ends = lax.all_gather(local_end[None], 'ctx', axis=0, tiled=True)  7.29 us
  transfers between devices with their start and end apart: 1, of which 0 were waited for; matrix products, arithmetic and copies ran while one was open for 1% of the time, Pallas kernels for 0%

profile of v2, /device:TPU:0, one launch (start us, length us, event | category | flops | bytes accessed | tf_op | source)
XLA Modules:
  0.0 319.1 jit_solution(2686972227091916919)
XLA Ops:
  0.0 0.7 slice_bitcast_fusion.2
  0.7 0.7 slice_bitcast_fusion
  1.5 2.4 collective-permute-start
  3.9 0.8 bitcast_negate_fusion
  4.7 1.5 multiply_bitcast_fusion.gain_ref
  6.3 0.0 collective-permute-done
  6.3 0.0 copy-start.3
  6.3 0.0 copy-start
  6.3 1.9 copy-done
  8.2 0.0 copy-start.1
  8.2 1.9 copy-done.1
  10.1 0.0 copy-start.2
  10.1 0.8 copy-done.2
  10.9 0.0 copy-start.4
  10.9 0.8 copy-done.4
  11.7 16.1 %segment_ends.1 = (f32[16,8,1024]{2,1,0:T(8,128)S(1)}, f32[16,1024]{1,0:T(8,128)S(1)}) custom-call(bf16[1536,1024]{1,0:T(8,128)(2,1)S(1)} %copy-done, bf16[1536,1024]{1,0:T(8,128)(2,1)S(1)} %copy-done.1, f32[3,2,1024]{2,1,0:T(2,128)S(1)} %convert_element_type.10.edge_ref, f32[3,3,1024]{2,1,0:T(4,128)S(1)} %copy-done.4, f32[16,1024]{1,0:T(8,128)S(1)} %bitcast.13), custom_call_target="tpu_custom_call" | custom-call | flops 50331648 | bytes 6291456 | tf_op jit(solution)/shard_map/segment_ends/pallas_call | solution.py:390
  27.8 0.0 copy-done.3
  27.8 0.0 copy-start.5
  27.8 0.8 copy-done.5
  28.6 7.3 %all-gather = f32[64,1024]{1,0:T(8,128)S(1)} all-gather(f32[16,1024]{1,0:T(8,128)S(1)} %get-tuple-element.8), channel_id=2, replica_groups=mesh['chan'=8,'ctx'=4] {'ctx'}, dimensions={0}, use_global_device_ids=true | all-gather | bytes 327680 | tf_op jit(solution)/shard_map/all_gather | solution.py:405
  35.9 0.7 multiply_reduce_fusion.carry_ref
  36.6 278.5 %mix.1 = bf16[1536,1024]{1,0:T(8,128)(2,1)} custom-call(bf16[1536,1024]{1,0:T(8,128)(2,1)} %q_ref.1, bf16[1536,1024]{1,0:T(8,128)(2,1)} %k_ref.3, bf16[1536,1024]{1,0:T(8,128)(2,1)} %v_ref.3, bf16[2048,1024]{1,0:T(8,128)(2,1)} %w_ref.1, f32[3,2,1024]{2,1,0:T(2,128)} %copy-done.3, f32[3,3,1024]{2,1,0:T(4,128)} %taps_ref.3, f32[16,1024]{1,0:T(8,128)} %bitcast.12, ...), custom_call_target="tpu_custom_call" | custom-call | flops 25870467072 | bytes 16777216 | tf_op jit(solution)/shard_map/mix/pallas_call | solution.py:415
  315.2 3.9 %copy.10 = bf16[1536,1024]{1,0:T(8,128)(2,1)} copy(bf16[1536,1024]{1,0:T(8,128)(2,1)} %mix.1) | data formatting | bytes 6291456
  (4 shorter events, 0.0 us)
Async XLA Ops:
  1.5 4.8 %collective-permute-start = (bf16[3,2,1024]{2,1,0:T(2,128)(2,1)S(1)}, bf16[3,2,1024]{2,1,0:T(2,128)(2,1)S(1)}, u32[]{:S(2)}, u32[]{:S(2)}) collective-permute-start(bf16[3,2,1024]{2,1,0:T(2,128)(2,1)S(1)} %pad_maximum_fusion), channel_id=1, source_target_pairs={{0,1},{1,2},{2,3},{4,5},{5,6},{6,7},{8,9},{9,10},{10,11},{12,13},{... | collective-permute-start | bytes 36872 | tf_op jit(solution)/shard_map/ppermute | solution.py:374
  6.3 21.5 %copy-start.3 = (f32[3,2,1024]{2,1,0:T(2,128)}, f32[3,2,1024]{2,1,0:T(2,128)S(1)}, u32[]{:S(2)}) copy-start(f32[3,2,1024]{2,1,0:T(2,128)S(1)} %convert_element_type.10.edge_ref) | copy-start | bytes 73732
  6.3 1.9 copy-start
  8.2 1.9 copy-start.1
  10.1 0.8 copy-start.2
  10.9 0.8 copy-start.4
  27.8 0.8 copy-start.5

commit v3 on v2

--- a/solution.py
+++ b/solution.py
@@ -44,13 +44,14 @@
     return put
 
 
-def ends_kernel(k_ref, v_ref, edge_ref, taps_ref, rate_ref, seg_ref, end_ref, padded, drive):
-    tokens = k_ref.shape[0]
-    modes = rate_ref.shape[0]
+def end_chunk(streams, edge_ref, taps_ref, rate, kept, seg_ref, end_ref, padded, drive):
+    tokens = drive.shape[0]
+    modes = rate.shape[0]
     length = tokens // SEGMENTS
+    k_ref, v_ref = streams
     short_stream(k_ref, edge_ref.at[1], taps_ref.at[1], padded, write_to(drive, length), length)
     short_stream(v_ref, edge_ref.at[2], taps_ref.at[2], padded, multiply_into(drive, length), length)
-    decay = jnp.exp(-rate_ref[...])
+    decay = jnp.exp(-rate)
     decays = [jnp.broadcast_to(decay[n : n + 1, :], (SEGMENTS, LANES)) for n in range(modes)]
     unroll = 4
 
@@ -64,29 +65,30 @@
     states = lax.fori_loop(0, length // unroll, steps, (zero,) * modes)
     for n in range(modes):
         seg_ref[n] = states[n]
-    span = jnp.exp(-rate_ref[...] * float(length))
+    span = jnp.exp(-rate * float(length))
     total = jnp.zeros((modes, LANES), jnp.float32)
     for seg in range(SEGMENTS):
         total = span * total + seg_ref[:, seg, :]
+        rows = slice(seg * length, (seg + 1) * length)
+        kept[rows, :] = drive[rows, :]
     end_ref[...] = total
 
 
 def gate_chunk(
-    streams, edge_ref, taps_ref, rate, gain, skip, seg_ref, carry,
+    q_ref, edge_ref, taps_ref, rate, gain, skip, seg_ref, carry, kept,
     out_ref, padded, drive, query, conv, starts,
 ):
     tokens = drive.shape[0]
     modes = rate.shape[0]
     length = tokens // SEGMENTS
-    q_ref, k_ref, v_ref = streams
     short_stream(q_ref, edge_ref.at[0], taps_ref.at[0], padded, write_to(query, length), length)
-    short_stream(k_ref, edge_ref.at[1], taps_ref.at[1], padded, write_to(drive, length), length)
-    short_stream(v_ref, edge_ref.at[2], taps_ref.at[2], padded, multiply_into(drive, length), length)
     span = jnp.exp(-rate * float(length))
     state = carry
     for seg in range(SEGMENTS):
         starts[:, seg, :] = state
         state = span * state + seg_ref[:, seg, :]
+        rows = slice(seg * length, (seg + 1) * length)
+        drive[rows, :] = kept[rows, :]
     decay = jnp.exp(-rate)
     decays = [jnp.broadcast_to(decay[n : n + 1, :], (SEGMENTS, LANES)) for n in range(modes)]
     gains = [jnp.broadcast_to(gain[n : n + 1, :], (SEGMENTS, LANES)) for n in range(modes)]
@@ -153,8 +155,8 @@
 
 def mix_kernel(
     shards, blocks, q_ref, k_ref, v_ref, w_ref, edge_ref, taps_ref, rate_ref, gain_ref, skip_ref,
-    seg_ref, carry_ref, out_ref, held, weight, total, streams, padded, drive, query, conv, starts,
-    in_sem, wown_sem, send_sem, recv_sem, wsend_sem, wrecv_sem,
+    out_ref, held, weight, total, streams, padded, drive, query, conv, starts, segs, ends,
+    in_sem, esend_sem, erecv_sem, wown_sem, send_sem, recv_sem, wsend_sem, wrecv_sem,
 ):
     tokens, channels = q_ref.shape
     depth, columns = w_ref.shape
@@ -183,17 +185,19 @@
     def block_of(index):
         return weight.at[pl.ds(pl.multiple_of(index * depth, depth), depth), :]
 
-    def fetch(chunk, act):
+    def fetch(chunk, names, act):
         slot = chunk % 2
         lanes = pl.ds(pl.multiple_of(chunk * LANES, LANES), LANES)
-        for which, ref in enumerate((q_ref, k_ref, v_ref)):
+        for which in names:
             act(
                 pltpu.make_async_copy(
-                    ref.at[:, lanes], streams.at[slot, which], in_sem.at[slot, which]
+                    (q_ref, k_ref, v_ref)[which].at[:, lanes],
+                    streams.at[slot, which],
+                    in_sem.at[slot, which],
                 )
             )
 
-    fetch(0, lambda copy: copy.start())
+    fetch(0, (0, 1, 2), lambda copy: copy.start())
     weight_copy = pltpu.make_async_copy(w_ref, block_of(ctx), wown_sem)
     weight_copy.start()
 
@@ -209,10 +213,10 @@
 
     pl.semaphore_signal(barrier, inc=1, device_id={"chan": targets[2]}, device_id_type=MESH)
     partners = [1] + list(range(2, blocks, 2))
-    for by in partners:
+    for by in range(1, blocks):
         pl.semaphore_signal(barrier, inc=1, device_id={"ctx": flip(by)}, device_id_type=MESH)
     lines = jnp.where(z > 0, 1, 0) + jnp.where(z < line - 1, 1, 0)
-    pl.semaphore_wait(barrier, lines + 1 + len(partners))
+    pl.semaphore_wait(barrier, lines + blocks)
 
     def piece_copy(shard, piece, way):
         part = held.at[shard, piece]
@@ -250,32 +254,89 @@
     for copy in first_sends:
         copy.start()
 
-    @pl.loop(0, chunks)
-    def _(chunk):
+    def ends_copy(source, piece, by):
+        part = ends.at[source, piece]
+        return pltpu.make_async_remote_copy(
+            src_ref=part,
+            dst_ref=part,
+            send_sem=esend_sem.at[piece, by],
+            recv_sem=erecv_sem.at[source, piece],
+            device_id={"ctx": flip(by)},
+            device_id_type=MESH,
+        )
+
+    def places(piece, sub):
+        chunk = piece * per_piece + sub
+        lanes = pl.ds(pl.multiple_of(chunk * LANES, LANES), LANES)
+        inside = pl.ds(pl.multiple_of(sub * LANES, LANES), LANES)
+        return chunk, lanes, inside
+
+    def advance(chunk, names):
         @pl.when(chunk < chunks - 1)
         def _():
-            fetch(chunk + 1, lambda copy: copy.start())
-
-        fetch(chunk, lambda copy: copy.wait())
-        piece = chunk // per_piece
-        lanes = pl.ds(pl.multiple_of(chunk * LANES, LANES), LANES)
-        inside = pl.ds(pl.multiple_of((chunk % per_piece) * LANES, LANES), LANES)
-        gate_chunk(
-            [streams.at[chunk % 2, which] for which in range(3)],
-            edge_ref.at[:, :, lanes],
-            taps_ref.at[:, :, lanes],
-            rate_ref[:, lanes],
-            gain_ref[:, lanes],
-            skip_ref[:, lanes],
-            seg_ref.at[:, :, lanes],
-            carry_ref[:, lanes],
-            held.at[me, piece, :, inside],
-            padded, drive, query, conv, starts,
-        )
-
-        @pl.when(chunk % per_piece == per_piece - 1)
+            fetch(chunk + 1, names, lambda copy: copy.start())
+
+        fetch(chunk, names, lambda copy: copy.wait())
+
+    def end_piece(piece):
+        @pl.loop(0, per_piece)
+        def _(sub):
+            chunk, lanes, inside = places(piece, sub)
+            advance(chunk, (1, 2))
+            end_chunk(
+                [streams.at[chunk % 2, 1], streams.at[chunk % 2, 2]],
+                edge_ref.at[:, :, lanes],
+                taps_ref.at[:, :, lanes],
+                rate_ref[:, lanes],
+                total.at[:, lanes],
+                segs.at[:, :, lanes],
+                ends.at[ctx, piece, :, inside],
+                padded, drive,
+            )
+
+        for by in range(1, blocks):
+            ends_copy(ctx, piece, by).start()
+
+    def gate_piece(piece):
+        for by in range(1, blocks):
+            ends_copy(flip(by), piece, by).wait_recv()
+
+        @pl.loop(0, per_piece)
+        def _(sub):
+            chunk, lanes, inside = places(piece, sub)
+            advance(chunk, (0,))
+            rate = rate_ref[:, lanes]
+            carry = jnp.zeros(rate.shape, jnp.float32)
+            for source in range(blocks):
+                hops = ctx - 1 - source
+                span = (tokens * jnp.maximum(hops, 0)).astype(jnp.float32)
+                part = jnp.exp(-rate * span) * ends[source, piece, :, inside]
+                carry = carry + jnp.where(hops >= 0, part, 0.0)
+            gate_chunk(
+                streams.at[chunk % 2, 0],
+                edge_ref.at[:, :, lanes],
+                taps_ref.at[:, :, lanes],
+                rate,
+                gain_ref[:, lanes],
+                skip_ref[:, lanes],
+                segs.at[:, :, lanes],
+                carry,
+                total.at[:, lanes],
+                held.at[me, piece, :, inside],
+                padded, drive, query, conv, starts,
+            )
+
+        onward(codes[0], piece, lambda copy: copy.start())
+
+    @pl.loop(0, PIECES + 1)
+    def _(step):
+        @pl.when(step < PIECES)
         def _():
-            onward(codes[0], piece, lambda copy: copy.start())
+            end_piece(step)
+
+        @pl.when(step >= 1)
+        def _():
+            gate_piece(step - 1)
 
     def zero_rows(at):
         total[pl.ds(pl.multiple_of(at * 64, 64), 64), :] = jnp.zeros((64, columns), jnp.float32)
@@ -361,6 +422,9 @@
 
     for copy in first_sends + later_sends:
         copy.wait_send()
+    for piece in range(PIECES):
+        for by in range(1, blocks):
+            ends_copy(ctx, piece, by).wait_send()
 
 
 def on_device(query_in, key_in, value_in, short_filter, residue, decay_rate, skip_gain, out_weight):
@@ -369,7 +433,6 @@
     modes = decay_rate.shape[1]
     shards = lax.axis_size("chan")
     blocks = lax.axis_size("ctx")
-    position = lax.axis_index("ctx")
     edge = jnp.stack([x[tokens - (tap_count - 1) :, :] for x in (query_in, key_in, value_in)])
     edge = lax.ppermute(edge, "ctx", [(i, i + 1) for i in range(blocks - 1)])
     edge = edge.astype(jnp.float32)
@@ -377,45 +440,15 @@
     gain = (residue * jnp.sqrt(decay_rate)).T
     skip = skip_gain[None, :]
 
-    stream = pl.BlockSpec((tokens, LANES), lambda i: (0, i))
-    edges = pl.BlockSpec((3, tap_count - 1, LANES), lambda i: (0, 0, i))
-    taps = pl.BlockSpec((3, tap_count, LANES), lambda i: (0, 0, i))
-    mode = pl.BlockSpec((modes, LANES), lambda i: (0, i))
-    segs = pl.BlockSpec((modes, SEGMENTS, LANES), lambda i: (0, 0, i))
     flat = pltpu.VMEM((tokens, LANES), jnp.float32)
     pad = pltpu.VMEM((tokens + HALO, LANES), jnp.float32)
-    chunks = channels // LANES
     work = tokens * channels * modes
-
-    segment_ends, local_end = pl.pallas_call(
-        ends_kernel,
-        grid=(chunks,),
-        in_specs=[stream, stream, edges, taps, mode],
-        out_specs=[segs, mode],
-        out_shape=[
-            jax.ShapeDtypeStruct((modes, SEGMENTS, channels), jnp.float32),
-            jax.ShapeDtypeStruct((modes, channels), jnp.float32),
-        ],
-        scratch_shapes=[pad, flat],
-        compiler_params=pltpu.CompilerParams(vmem_limit_bytes=32 * MIB),
-        cost_estimate=pl.CostEstimate(flops=2 * work, bytes_accessed=4 * tokens * channels, transcendentals=0),
-        name="segment_ends",
-    )(key_in, value_in, edge, short_filter, rate)
-
-    ends = lax.all_gather(local_end[None], "ctx", axis=0, tiled=True)
-    hops = position - 1 - jnp.arange(blocks)
-    span = (tokens * jnp.maximum(hops, 0)).astype(jnp.float32)
-    weights = jnp.where(
-        (hops >= 0)[:, None, None], jnp.exp(-rate[None] * span[:, None, None]), 0.0
-    )
-    carry = jnp.sum(weights * ends, axis=0)
-
     depth, columns = out_weight.shape
     partners = blocks // 2
     return pl.pallas_call(
         functools.partial(mix_kernel, shards, blocks),
         in_specs=[pl.BlockSpec(memory_space=pl.ANY)] * 4
-        + [pl.BlockSpec(memory_space=pltpu.VMEM)] * 7,
+        + [pl.BlockSpec(memory_space=pltpu.VMEM)] * 5,
         out_specs=pl.BlockSpec(memory_space=pltpu.VMEM),
         out_shape=jax.ShapeDtypeStruct((tokens, columns), jnp.bfloat16),
         scratch_shapes=[
@@ -428,7 +461,11 @@
             flat,
             flat,
             pltpu.VMEM((modes, SEGMENTS, LANES), jnp.float32),
+            pltpu.VMEM((modes, SEGMENTS, channels), jnp.float32),
+            pltpu.VMEM((blocks, PIECES, modes, channels // PIECES), jnp.float32),
             pltpu.SemaphoreType.DMA((2, 3)),
+            pltpu.SemaphoreType.DMA((PIECES, blocks)),
+            pltpu.SemaphoreType.DMA((blocks, PIECES)),
             pltpu.SemaphoreType.DMA,
             pltpu.SemaphoreType.DMA((shards, PIECES, 3)),
             pltpu.SemaphoreType.DMA((shards, PIECES)),
@@ -439,14 +476,13 @@
             collective_id=0, has_side_effects=True, vmem_limit_bytes=62 * MIB
         ),
         cost_estimate=pl.CostEstimate(
-            flops=2 * tokens * shards * channels * columns + 4 * work,
+            flops=2 * tokens * shards * channels * columns + 6 * work,
             bytes_accessed=6 * tokens * channels + 2 * depth * columns + 2 * tokens * columns,
             transcendentals=0,
         ),
         name="mix",
     )(
         query_in, key_in, value_in, out_weight, edge, short_filter, rate, gain, skip,
-        segment_ends, carry,
     )
 
 

time: 320 us -> 381 us (1.19)
  Pallas kernels: 295 us -> 371 us
  blocking collectives: 7.29 us -> 0 us
  local copies, waits for them, and re-layouts: 11.5 us -> 5.33 us
    pallas_call x1, Pallas kernels: 279 us -> 371 us  [on_device(): pl.pallas_call(functools.partial(mix_kernel, shards, blocks), in_specs=[p...]
    pallas_call x1 -> x0, Pallas kernels: 16.1 us -> none  [on_device(): pl.pallas_call(ends_kernel, grid=(chunks,), in_specs=[stream, stream, edg...]
    all_gather x1 -> x0, blocking collectives: 7.29 us -> none  [on_device(): ends = lax.all_gather(local_end[None], 'ctx', axis=0, tiled=True)]
    unnamed x13 -> x1, local copies, waits for them, and re-layouts: 10.1 us -> 3.86 us
  transfers between devices with their start and end apart: 1 -> 1, of which waited for: 0 -> 0; matrix products, arithmetic and copies ran while one was open for 1% -> 0% of each run, Pallas kernels for 0% -> 0%
where the time goes in v3:
time: 381 us
  Pallas kernels  371 us (97%)
  local copies, waits for them, and re-layouts  5.33 us (1%)
    pallas_call x1, Pallas kernels, on_device(): pl.pallas_call(functools.partial(mix_kernel, shards, blocks), in_specs=[p...  371 us
  transfers between devices with their start and end apart: 1, of which 0 were waited for; matrix products, arithmetic and copies ran while one was open for 0% of the time, Pallas kernels for 0%

profile of v3, /device:TPU:0, one launch (start us, length us, event | category | flops | bytes accessed | tf_op | source)
XLA Modules:
  0.0 380.8 jit_solution(3898620764595205621)
XLA Ops:
  0.0 0.7 slice_bitcast_fusion.2
  0.7 0.7 slice_bitcast_fusion
  1.5 2.4 collective-permute-start
  3.9 1.5 multiply_bitcast_fusion.gain_ref
  5.4 0.0 collective-permute-done
  5.4 0.6 convert_element_type.3.edge_ref
  6.0 370.9 %mix.1 = bf16[1536,1024]{1,0:T(8,128)(2,1)} custom-call(bf16[1536,1024]{1,0:T(8,128)(2,1)} %q_ref.1, bf16[1536,1024]{1,0:T(8,128)(2,1)} %k_ref.1, bf16[1536,1024]{1,0:T(8,128)(2,1)} %v_ref.1, bf16[2048,1024]{1,0:T(8,128)(2,1)} %w_ref.1, f32[3,2,1024]{2,1,0:T(2,128)} %convert_element_type.3.edge_ref, f32[3,3,1024]{2,1,0:T(4,128)} %taps_ref.1, ...), custom_call_target="tpu_custom_call" | custom-call | flops 25920798720 | bytes 16777216 | tf_op jit(solution)/shard_map/mix/pallas_call | solution.py:448
  376.9 3.9 %copy.10 = bf16[1536,1024]{1,0:T(8,128)(2,1)} copy(bf16[1536,1024]{1,0:T(8,128)(2,1)} %mix.1) | data formatting | bytes 6291456
  (1 shorter events, 0.0 us)
Async XLA Ops:
  1.5 3.9 %collective-permute-start = (bf16[3,2,1024]{2,1,0:T(2,128)(2,1)S(1)}, bf16[3,2,1024]{2,1,0:T(2,128)(2,1)S(1)}, u32[]{:S(2)}, u32[]{:S(2)}) collective-permute-start(bf16[3,2,1024]{2,1,0:T(2,128)(2,1)S(1)} %pad_maximum_fusion), channel_id=1, source_target_pairs={{0,1},{1,2},{2,3},{4,5},{5,6},{6,7},{8,9},{9,10},{10,11},{12,13},{... | collective-permute-start | bytes 36872 | tf_op jit(solution)/shard_map/ppermute | solution.py:437

commit v4 on v3

--- a/solution.py
+++ b/solution.py
@@ -249,11 +249,6 @@
             def _(way=way):
                 act(piece_copy(shard, piece, way))
 
-    weight_copy.wait()
-    first_sends = [weight_send(ctx, by, slot) for slot, by in enumerate(partners)]
-    for copy in first_sends:
-        copy.start()
-
     def ends_copy(source, piece, by):
         part = ends.at[source, piece]
         return pltpu.make_async_remote_copy(
@@ -338,6 +333,11 @@
         def _():
             gate_piece(step - 1)
 
+    weight_copy.wait()
+    first_sends = [weight_send(ctx, by, slot) for slot, by in enumerate(partners)]
+    for copy in first_sends:
+        copy.start()
+
     def zero_rows(at):
         total[pl.ds(pl.multiple_of(at * 64, 64), 64), :] = jnp.zeros((64, columns), jnp.float32)
 
@@ -350,28 +350,17 @@
     half = shards // 2
     later_sends = []
     for k in range(1, half):
-        code = codes[k]
-        if k < half - 1:
-
-            @pl.loop(0, PIECES)
-            def _(piece, code=code):
-                arrive(code, piece)
-        else:
-
-            @pl.loop(0, PIECES // 2)
-            def _(piece, code=code):
-                arrive(code, piece)
-
-            for by in partners[1:]:
-                block = flip(by)
-                weight_send(block, 1, 0).wait_recv()
-                copy = weight_send(block, 1, len(partners) + len(later_sends))
-                copy.start()
-                later_sends.append(copy)
-
-            @pl.loop(PIECES // 2, PIECES)
-            def _(piece, code=code):
-                arrive(code, piece)
+
+        @pl.loop(0, PIECES)
+        def _(piece, code=codes[k]):
+            arrive(code, piece)
+
+    for by in partners[1:]:
+        block = flip(by)
+        weight_send(block, 1, 0).wait_recv()
+        copy = weight_send(block, 1, len(partners) + len(later_sends))
+        copy.start()
+        later_sends.append(copy)
 
     weight_send(flip(1), 1, 0).wait_recv()
     for by in partners[1:]:

time: 381 us -> 300 us (0.79)
  Pallas kernels: 371 us -> 290 us
    pallas_call x1, Pallas kernels: 371 us -> 290 us  [on_device(): pl.pallas_call(functools.partial(mix_kernel, shards, blocks), in_specs=[p...]
  transfers between devices with their start and end apart: 1 -> 1, of which waited for: 0 -> 0; matrix products, arithmetic and copies ran while one was open for 0% -> 1% of each run, Pallas kernels for 0% -> 0%
where the time goes in v4:
time: 300 us
  Pallas kernels  290 us (97%)
  local copies, waits for them, and re-layouts  5.33 us (2%)
    pallas_call x1, Pallas kernels, on_device(): pl.pallas_call(functools.partial(mix_kernel, shards, blocks), in_specs=[p...  290 us
  transfers between devices with their start and end apart: 1, of which 0 were waited for; matrix products, arithmetic and copies ran while one was open for 1% of the time, Pallas kernels for 0%

profile of v4, /device:TPU:0, one launch (start us, length us, event | category | flops | bytes accessed | tf_op | source)
XLA Modules:
  0.0 299.6 jit_solution(12820052920689106786)
XLA Ops:
  0.0 0.7 slice_bitcast_fusion.2
  0.7 0.7 slice_bitcast_fusion
  1.5 2.4 collective-permute-start
  3.9 1.5 multiply_bitcast_fusion.gain_ref
  5.4 0.0 collective-permute-done
  5.4 0.6 convert_element_type.3.edge_ref
  6.0 289.7 %mix.1 = bf16[1536,1024]{1,0:T(8,128)(2,1)} custom-call(bf16[1536,1024]{1,0:T(8,128)(2,1)} %q_ref.1, bf16[1536,1024]{1,0:T(8,128)(2,1)} %k_ref.1, bf16[1536,1024]{1,0:T(8,128)(2,1)} %v_ref.1, bf16[2048,1024]{1,0:T(8,128)(2,1)} %w_ref.1, f32[3,2,1024]{2,1,0:T(2,128)} %convert_element_type.3.edge_ref, f32[3,3,1024]{2,1,0:T(4,128)} %taps_ref.1, ...), custom_call_target="tpu_custom_call" | custom-call | flops 25920798720 | bytes 16777216 | tf_op jit(solution)/shard_map/mix/pallas_call | solution.py:437
  295.7 3.9 %copy.10 = bf16[1536,1024]{1,0:T(8,128)(2,1)} copy(bf16[1536,1024]{1,0:T(8,128)(2,1)} %mix.1) | data formatting | bytes 6291456
  (1 shorter events, 0.0 us)
Async XLA Ops:
  1.5 3.9 %collective-permute-start = (bf16[3,2,1024]{2,1,0:T(2,128)(2,1)S(1)}, bf16[3,2,1024]{2,1,0:T(2,128)(2,1)S(1)}, u32[]{:S(2)}, u32[]{:S(2)}) collective-permute-start(bf16[3,2,1024]{2,1,0:T(2,128)(2,1)S(1)} %pad_maximum_fusion), channel_id=1, source_target_pairs={{0,1},{1,2},{2,3},{4,5},{5,6},{6,7},{8,9},{9,10},{10,11},{12,13},{... | collective-permute-start | bytes 36872 | tf_op jit(solution)/shard_map/ppermute | solution.py:426
